TPU v7x, 32 devices: a whole 2x2x4 slice. The times are simulated.
32 devices in a mesh: gx: 16 (over z, y, core), gy: 2 (over x).
Axes of the slice: x: 2, y: 2, z: 4, core: 2. Of those that a mesh axis runs over, the one named last changes fastest.
Arguments:
- source: float32 [64, 64, 256], P('gx', 'gy'), may hold values from -96 to 96
- region: int32 [64, 64, 256], P('gx', 'gy'), may hold values from 0 to 63
- permeability: float32 [64], replicated, may hold values from 0.1 to 10
- owners: int32 [16, 2], P('gx'), may hold values from 0 to 1
Outputs:
- pressure: float32 [64, 64, 256], P('gx', 'gy')
All inputs are finite; a program needn't handle non-finite values.
Results may differ from a plain program's by a relative error of at most 0.0001.
Values sent between devices are 32-bit elements; how exact they have to be, the bound alone decides.
A program may use at most 64 MiB of HBM per device.

v0:
```python
import jax
import jax.numpy as jnp
from jax import lax
from jax.sharding import PartitionSpec as P

POST_SWEEPS = 2
COARSE_SWEEPS = 6


RELAX_WEIGHT = 0.6
MASS_TERM = 0.1


def extended(cells, sides, width):
    for axis, dim in sides:
        count = lax.axis_size(axis)
        ends = count - 1
        head = lax.slice_in_dim(cells, 0, width, axis=dim)
        tail = lax.slice_in_dim(cells, cells.shape[dim] - width, cells.shape[dim], axis=dim)
        cells = jnp.concatenate(
            [
                lax.ppermute(tail, axis, [(i, (i + 1) % count) for i in range(ends)]),
                cells,
                lax.ppermute(head, axis, [((i + 1) % count, i) for i in range(ends)]),
            ],
            axis=dim,
        )
    return cells


def stencil_sum(padded):
    blended = 0.5 * padded[:-2] + padded[1:-1] + 0.5 * padded[2:]
    blended = 0.5 * blended[:, :-2] + blended[:, 1:-1] + 0.5 * blended[:, 2:]
    blended = 0.5 * blended[:, :, :-2] + blended[:, :, 1:-1] + 0.5 * blended[:, :, 2:]
    return 2.0 * (blended - padded[1:-1, 1:-1, 1:-1])


def pad_all(values):
    return jnp.pad(values, 1)


def pad_depth(values):
    return jnp.pad(values, ((0, 0), (0, 0), (1, 1)))


def fine_rims(values):
    return pad_depth(extended(values, (("gx", 0), ("gy", 1)), 1))


def operate(values, conduct, cond_pad, diagonal, factor, extend):
    value_pad = extend(values)
    return diagonal * values - factor * (
        conduct * stencil_sum(value_pad) + stencil_sum(cond_pad * value_pad)
    )


def coarsen(values):
    size_x, size_y, size_z = values.shape
    return values.reshape(size_x // 2, 2, size_y // 2, 2, size_z // 2, 2).mean(axis=(1, 3, 5))


def local_ratio(numer, denom):
    return jnp.sum(numer) / jnp.maximum(jnp.sum(denom), 1.0)


def coarse_sweeps(residual, conduct, cond_pad, region_mask, extend, totals):
    diagonal = MASS_TERM + 0.125 * (14.0 * conduct + stencil_sum(cond_pad))
    correction = jnp.zeros_like(residual)
    for iteration in range(COARSE_SWEEPS):
        applied = operate(correction, conduct, cond_pad, diagonal, 0.125, extend)
        correction = region_mask * (correction + RELAX_WEIGHT * (residual - applied) / diagonal)
    applied = operate(correction, conduct, cond_pad, diagonal, 0.125, extend)
    ratio = totals(region_mask * (residual - applied), region_mask * diagonal)
    return correction + region_mask * ratio


def lookup_table(region, permeability):
    labels = jnp.arange(permeability.shape[0], dtype=jnp.int32)[:, None, None, None]
    matches = region[None] == labels
    return jnp.sum(jnp.where(matches, permeability[:, None, None, None], 0.0), axis=0)


def on_device(source, region, permeability, owners):
    conduct = lookup_table(region, permeability)
    cond_pad = pad_depth(extended(conduct, (("gx", 0), ("gy", 1)), 1))
    diagonal = MASS_TERM + 0.5 * (14.0 * conduct + stencil_sum(cond_pad))

    def relax(pressure):
        applied = operate(pressure, conduct, cond_pad, diagonal, 0.5, fine_rims)
        return pressure + RELAX_WEIGHT * (source - applied) / diagonal

    pressure = RELAX_WEIGHT * source / diagonal
    pressure = relax(pressure)
    residual = source - operate(pressure, conduct, cond_pad, diagonal, 0.5, fine_rims)
    coarse_res = coarsen(residual)
    coarse_cond = coarsen(conduct)
    size_x, size_y, size_z = coarse_res.shape
    my_index = lax.axis_index("gy")
    owner_row = owners[0]
    my_owner = owner_row[my_index]
    group_res, group_cond = (
        lax.all_gather(coarse_res, "gy", axis=1, tiled=True),
        lax.all_gather(coarse_cond, "gy", axis=1, tiled=True),
    )
    owned = (owner_row == my_owner).astype(jnp.float32)
    region_mask = jnp.repeat(owned, size_y)[None, :, None]
    group_cond = group_cond * region_mask
    stacked = coarse_sweeps(
        group_res * region_mask, group_cond, pad_all(group_cond), region_mask, pad_all, local_ratio
    )
    correction = lax.dynamic_slice_in_dim(stacked, my_index * size_y, size_y, 1)
    fine_corr = jnp.broadcast_to(
        correction[:, None, :, None, :, None], (size_x, 2, size_y, 2, size_z, 2)
    ).reshape(source.shape)
    pressure = pressure + fine_corr
    for iteration in range(POST_SWEEPS):
        pressure = relax(pressure)
    return pressure


def solution(mesh):
    placed = (P("gx", "gy", None), P("gx", "gy", None), P(), P("gx", None))
    return jax.shard_map(
        on_device, mesh=mesh, in_specs=placed, out_specs=P("gx", "gy", None), check_vma=False
    )
```

profile of v0, /device:TPU:1, one launch (start us, length us, event | category | flops | bytes accessed | tf_op | source)
XLA Modules:
  0.0 134.1 jit_solution(6501710380920065260)
XLA Ops:
  0.0 1.9 %select_reduce_fusion = f32[4,32,256]{2,1,0:T(8,128)S(1)} fusion(f32[64]{0:T(128)} %param.6, s32[4,32,256]{2,1,0:T(8,128)} %param.5), kind=kLoop, calls=%fused_computation | loop fusion | flops 6258688 | bytes 262400 | tf_op jit(solution)/shard_map/reduce_sum | solution.py:80
  1.9 4.5 %collective-permute-start = (f32[1,32,256]{2,1,0:T(8,128)S(1)}, f32[1,32,256]{2,1,0:T(8,128)S(1)}, u32[]{:S(2)}, u32[]{:S(2)}) collective-permute-start(f32[1,32,256]{2,1,0:T(8,128)S(1)} %get-tuple-element.37), channel_id=1, source_target_pairs={{0,2},{2,4},{4,6},{6,8},{8,10},{10,12},{12,14},{14,16},{16,18},{18... | collective-permute-start | bytes 98312 | tf_op jit(solution)/shard_map/ppermute | solution.py:22
  6.4 1.9 %collective-permute-start.1 = (f32[1,32,256]{2,1,0:T(8,128)S(1)}, f32[1,32,256]{2,1,0:T(8,128)S(1)}, u32[]{:S(2)}, u32[]{:S(2)}) collective-permute-start(f32[1,32,256]{2,1,0:T(8,128)S(1)} %get-tuple-element.38), channel_id=1, source_target_pairs={{2,0},{4,2},{6,4},{8,6},{10,8},{12,10},{14,12},{16,14},{18,16},{20... | collective-permute-start | bytes 98312 | tf_op jit(solution)/shard_map/ppermute | solution.py:24
  8.4 9.8 %reshape.27 = f32[2,2,16,2,128,2]{5,4,3,2,1,0:T(8,128)} reshape(f32[4,32,256]{2,1,0:T(8,128)S(1)} %select_reduce_fusion) | data formatting | bytes 262144 | tf_op jit(solution)/shard_map/reshape | solution.py:59
  18.2 4.0 %reduce_sum.47 = f32[2,16,128]{2,1,0:T(8,128)S(1)} reduce(f32[2,2,16,2,128,2]{5,4,3,2,1,0:T(8,128)} %reshape.27, f32[]{:T(128)} %constant.14.clone.1), dimensions={1,3,5}, to_apply=%region_2.3 | reduce | flops 28672 | bytes 147460 | tf_op jit(solution)/shard_map/reduce_sum | solution.py:59
  22.2 0.6 constant_dynamic-slice_fusion
  22.8 0.6 fusion.213
  23.6 0.1 mul.792
  23.7 3.1 %collective-permute-start.2 = (f32[6,1,256]{2,1,0:T(1,128)S(1)}, f32[6,1,256]{2,1,0:T(1,128)S(1)}, u32[]{:S(2)}, u32[]{:S(2)}) collective-permute-start(f32[6,1,256]{2,1,0:T(1,128)S(1)} %get-tuple-element.27), channel_id=1, source_target_pairs={{0,1},{2,3},{4,5},{6,7},{8,9},{10,11},{12,13},{14,15},{16,17},{18,... | collective-permute-start | bytes 18440 | tf_op jit(solution)/shard_map/ppermute | solution.py:22
  26.8 1.3 collective-permute-start.3
  28.1 3.9 %all_gather.7 = f32[2,32,128]{2,1,0:T(8,128)S(1)} all-gather(f32[2,16,128]{2,1,0:T(8,128)S(1)} %broadcast_multiply_fusion.1), channel_id=1, replica_groups=mesh['gx'=16,'gy'=2] {'gy'}, dimensions={1}, use_global_device_ids=true | all-gather | bytes 49152 | tf_op jit(solution)/shard_map/all_gather | solution.py:103
  32.0 0.2 select_maximum_fusion.16
  32.3 0.2 multiply_divide_fusion
  32.4 5.1 %collective-permute-start.4 = (f32[1,32,256]{2,1,0:T(8,128)S(1)}, f32[1,32,256]{2,1,0:T(8,128)S(1)}, u32[]{:S(2)}, u32[]{:S(2)}) collective-permute-start(f32[1,32,256]{2,1,0:T(8,128)S(1)} %get-tuple-element.35), channel_id=1, source_target_pairs={{0,2},{2,4},{4,6},{6,8},{8,10},{10,12},{12,14},{14,16},{16,18},{18... | collective-permute-start | bytes 98312 | tf_op jit(solution)/shard_map/ppermute | solution.py:22
  37.5 1.9 %collective-permute-start.5 = (f32[1,32,256]{2,1,0:T(8,128)S(1)}, f32[1,32,256]{2,1,0:T(8,128)S(1)}, u32[]{:S(2)}, u32[]{:S(2)}) collective-permute-start(f32[1,32,256]{2,1,0:T(8,128)S(1)} %get-tuple-element.36), channel_id=1, source_target_pairs={{2,0},{4,2},{6,4},{8,6},{10,8},{12,10},{14,12},{16,14},{18,16},{20... | collective-permute-start | bytes 98312 | tf_op jit(solution)/shard_map/ppermute | solution.py:24
  39.5 3.2 %collective-permute-done.5 = f32[1,32,256]{2,1,0:T(8,128)S(1)} collective-permute-done((f32[1,32,256]{2,1,0:T(8,128)S(1)}, f32[1,32,256]{2,1,0:T(8,128)S(1)}, u32[]{:S(2)}, u32[]{:S(2)}) %collective-permute-start.5) | collective-permute-done | bytes 32800 | tf_op jit(solution)/shard_map/ppermute | solution.py:24
  42.8 3.7 %collective-permute-start.6 = (f32[6,1,256]{2,1,0:T(1,128)S(1)}, f32[6,1,256]{2,1,0:T(1,128)S(1)}, u32[]{:S(2)}, u32[]{:S(2)}) collective-permute-start(f32[6,1,256]{2,1,0:T(1,128)S(1)} %get-tuple-element.25), channel_id=1, source_target_pairs={{0,1},{2,3},{4,5},{6,7},{8,9},{10,11},{12,13},{14,15},{16,17},{18,... | collective-permute-start | bytes 18440 | tf_op jit(solution)/shard_map/ppermute | solution.py:22
  46.5 1.3 collective-permute-start.7
  47.8 0.2 multiply_add_fusion.12
  48.0 2.8 %collective-permute-done.7 = f32[6,1,256]{2,1,0:T(1,128)S(1)} collective-permute-done((f32[6,1,256]{2,1,0:T(1,128)S(1)}, f32[6,1,256]{2,1,0:T(1,128)S(1)}, u32[]{:S(2)}, u32[]{:S(2)}) %collective-permute-start.7) | collective-permute-done | bytes 6176 | tf_op jit(solution)/shard_map/ppermute | solution.py:24
  50.8 0.3 select_maximum_fusion.12
  51.4 0.3 fusion.62
  51.7 3.3 %collective-permute-start.8 = (f32[1,32,256]{2,1,0:T(8,128)S(1)}, f32[1,32,256]{2,1,0:T(8,128)S(1)}, u32[]{:S(2)}, u32[]{:S(2)}) collective-permute-start(f32[1,32,256]{2,1,0:T(8,128)S(1)} %get-tuple-element.33), channel_id=1, source_target_pairs={{0,2},{2,4},{4,6},{6,8},{8,10},{10,12},{12,14},{14,16},{16,18},{18... | collective-permute-start | bytes 98312 | tf_op jit(solution)/shard_map/ppermute | solution.py:22
  55.0 1.9 %collective-permute-start.9 = (f32[1,32,256]{2,1,0:T(8,128)S(1)}, f32[1,32,256]{2,1,0:T(8,128)S(1)}, u32[]{:S(2)}, u32[]{:S(2)}) collective-permute-start(f32[1,32,256]{2,1,0:T(8,128)S(1)} %get-tuple-element.34), channel_id=1, source_target_pairs={{2,0},{4,2},{6,4},{8,6},{10,8},{12,10},{14,12},{16,14},{18,16},{20... | collective-permute-start | bytes 98312 | tf_op jit(solution)/shard_map/ppermute | solution.py:24
  57.0 3.5 %collective-permute-done.9 = f32[1,32,256]{2,1,0:T(8,128)S(1)} collective-permute-done((f32[1,32,256]{2,1,0:T(8,128)S(1)}, f32[1,32,256]{2,1,0:T(8,128)S(1)}, u32[]{:S(2)}, u32[]{:S(2)}) %collective-permute-start.9) | collective-permute-done | bytes 32800 | tf_op jit(solution)/shard_map/ppermute | solution.py:24
  60.5 1.7 %collective-permute-start.10 = (f32[6,1,256]{2,1,0:T(1,128)S(1)}, f32[6,1,256]{2,1,0:T(1,128)S(1)}, u32[]{:S(2)}, u32[]{:S(2)}) collective-permute-start(f32[6,1,256]{2,1,0:T(1,128)S(1)} %get-tuple-element.23), channel_id=1, source_target_pairs={{0,1},{2,3},{4,5},{6,7},{8,9},{10,11},{12,13},{14,15},{16,17},{18,... | collective-permute-start | bytes 18440 | tf_op jit(solution)/shard_map/ppermute | solution.py:22
  62.2 1.3 collective-permute-start.11
  63.5 3.0 %collective-permute-done.11 = f32[6,1,256]{2,1,0:T(1,128)S(1)} collective-permute-done((f32[6,1,256]{2,1,0:T(1,128)S(1)}, f32[6,1,256]{2,1,0:T(1,128)S(1)}, u32[]{:S(2)}, u32[]{:S(2)}) %collective-permute-start.11) | collective-permute-done | bytes 6176 | tf_op jit(solution)/shard_map/ppermute | solution.py:24
  66.6 0.3 select_maximum_fusion.8
  67.1 0.3 fusion.49
  67.4 9.8 %reshape.26 = f32[2,2,16,2,128,2]{5,4,3,2,1,0:T(8,128)} reshape(f32[4,32,256]{2,1,0:T(8,128)S(1)} %fusion.49) | data formatting | bytes 262144 | tf_op jit(solution)/shard_map/reshape | solution.py:59
  77.2 4.0 %reduce_sum.46 = f32[2,16,128]{2,1,0:T(8,128)S(1)} reduce(f32[2,2,16,2,128,2]{5,4,3,2,1,0:T(8,128)} %reshape.26, f32[]{:T(128)} %constant.14.clone.1), dimensions={1,3,5}, to_apply=%region_1.2 | reduce | flops 28672 | bytes 147460 | tf_op jit(solution)/shard_map/reduce_sum | solution.py:59
  81.2 3.3 %all_gather.6 = f32[2,32,128]{2,1,0:T(8,128)S(1)} all-gather(f32[2,16,128]{2,1,0:T(8,128)S(1)} %broadcast_multiply_fusion.2), channel_id=1, replica_groups=mesh['gx'=16,'gy'=2] {'gy'}, dimensions={1}, use_global_device_ids=true | all-gather | bytes 49152 | tf_op jit(solution)/shard_map/all_gather | solution.py:102
  84.5 0.1 fusion.207
  84.6 0.2 multiply_add_fusion.11
  84.9 0.1 fusion.208
  85.0 0.2 multiply_add_fusion.10
  85.3 0.1 fusion.209
  85.4 0.2 multiply_add_fusion.9
  85.6 0.1 fusion.210
  85.8 0.2 multiply_add_fusion.8
  86.0 0.1 fusion.211
  86.1 0.2 multiply_add_fusion.7
  86.4 0.1 fusion.212
  86.5 0.2 multiply_add_fusion.6
  86.8 0.8 multiply_reduce_fusion
  89.0 3.9 %broadcast_in_dim.31 = f32[2,2,16,2,128,2]{5,4,3,2,1,0:T(8,128)} broadcast(f32[2,16,128]{2,1,0:T(8,128)S(1)} %dynamic-slice_add_fusion), dimensions={0,2,4} | broadcast | bytes 147456 | tf_op jit(solution)/shard_map/broadcast_in_dim | solution.py:112
  92.9 6.9 %reshape.28 = f32[4,32,256]{2,1,0:T(8,128)S(1)} reshape(f32[2,2,16,2,128,2]{5,4,3,2,1,0:T(8,128)} %broadcast_in_dim.31) | data formatting | bytes 262144 | tf_op jit(solution)/shard_map/reshape | solution.py:114
  99.9 4.7 %collective-permute-start.12 = (f32[1,32,256]{2,1,0:T(8,128)S(1)}, f32[1,32,256]{2,1,0:T(8,128)S(1)}, u32[]{:S(2)}, u32[]{:S(2)}) collective-permute-start(f32[1,32,256]{2,1,0:T(8,128)S(1)} %get-tuple-element.31), channel_id=1, source_target_pairs={{0,2},{2,4},{4,6},{6,8},{8,10},{10,12},{12,14},{14,16},{16,18},{18... | collective-permute-start | bytes 98312 | tf_op jit(solution)/shard_map/ppermute | solution.py:22
  104.6 1.9 %collective-permute-start.13 = (f32[1,32,256]{2,1,0:T(8,128)S(1)}, f32[1,32,256]{2,1,0:T(8,128)S(1)}, u32[]{:S(2)}, u32[]{:S(2)}) collective-permute-start(f32[1,32,256]{2,1,0:T(8,128)S(1)} %get-tuple-element.32), channel_id=1, source_target_pairs={{2,0},{4,2},{6,4},{8,6},{10,8},{12,10},{14,12},{16,14},{18,16},{20... | collective-permute-start | bytes 98312 | tf_op jit(solution)/shard_map/ppermute | solution.py:24
  106.5 3.3 %collective-permute-done.13 = f32[1,32,256]{2,1,0:T(8,128)S(1)} collective-permute-done((f32[1,32,256]{2,1,0:T(8,128)S(1)}, f32[1,32,256]{2,1,0:T(8,128)S(1)}, u32[]{:S(2)}, u32[]{:S(2)}) %collective-permute-start.13) | collective-permute-done | bytes 32800 | tf_op jit(solution)/shard_map/ppermute | solution.py:24
  109.9 1.6 %collective-permute-start.14 = (f32[6,1,256]{2,1,0:T(1,128)S(1)}, f32[6,1,256]{2,1,0:T(1,128)S(1)}, u32[]{:S(2)}, u32[]{:S(2)}) collective-permute-start(f32[6,1,256]{2,1,0:T(1,128)S(1)} %get-tuple-element.21), channel_id=1, source_target_pairs={{0,1},{2,3},{4,5},{6,7},{8,9},{10,11},{12,13},{14,15},{16,17},{18,... | collective-permute-start | bytes 18440 | tf_op jit(solution)/shard_map/ppermute | solution.py:22
  111.5 1.3 collective-permute-start.15
  112.8 3.1 %collective-permute-done.15 = f32[6,1,256]{2,1,0:T(1,128)S(1)} collective-permute-done((f32[6,1,256]{2,1,0:T(1,128)S(1)}, f32[6,1,256]{2,1,0:T(1,128)S(1)}, u32[]{:S(2)}, u32[]{:S(2)}) %collective-permute-start.15) | collective-permute-done | bytes 6176 | tf_op jit(solution)/shard_map/ppermute | solution.py:24
  115.8 0.3 select_maximum_fusion.4
  116.4 0.3 fusion.39
  116.7 4.2 %collective-permute-start.16 = (f32[1,32,256]{2,1,0:T(8,128)S(1)}, f32[1,32,256]{2,1,0:T(8,128)S(1)}, u32[]{:S(2)}, u32[]{:S(2)}) collective-permute-start(f32[1,32,256]{2,1,0:T(8,128)S(1)} %get-tuple-element.29), channel_id=1, source_target_pairs={{0,2},{2,4},{4,6},{6,8},{8,10},{10,12},{12,14},{14,16},{16,18},{18... | collective-permute-start | bytes 98312 | tf_op jit(solution)/shard_map/ppermute | solution.py:22
  120.9 1.9 %collective-permute-start.17 = (f32[1,32,256]{2,1,0:T(8,128)S(1)}, f32[1,32,256]{2,1,0:T(8,128)S(1)}, u32[]{:S(2)}, u32[]{:S(2)}) collective-permute-start(f32[1,32,256]{2,1,0:T(8,128)S(1)} %get-tuple-element.30), channel_id=1, source_target_pairs={{2,0},{4,2},{6,4},{8,6},{10,8},{12,10},{14,12},{16,14},{18,16},{20... | collective-permute-start | bytes 98312 | tf_op jit(solution)/shard_map/ppermute | solution.py:24
  122.9 3.7 %collective-permute-done.17 = f32[1,32,256]{2,1,0:T(8,128)S(1)} collective-permute-done((f32[1,32,256]{2,1,0:T(8,128)S(1)}, f32[1,32,256]{2,1,0:T(8,128)S(1)}, u32[]{:S(2)}, u32[]{:S(2)}) %collective-permute-start.17) | collective-permute-done | bytes 32800 | tf_op jit(solution)/shard_map/ppermute | solution.py:24
  126.5 1.7 %collective-permute-start.18 = (f32[6,1,256]{2,1,0:T(1,128)S(1)}, f32[6,1,256]{2,1,0:T(1,128)S(1)}, u32[]{:S(2)}, u32[]{:S(2)}) collective-permute-start(f32[6,1,256]{2,1,0:T(1,128)S(1)} %get-tuple-element.19), channel_id=1, source_target_pairs={{0,1},{2,3},{4,5},{6,7},{8,9},{10,11},{12,13},{14,15},{16,17},{18,... | collective-permute-start | bytes 18440 | tf_op jit(solution)/shard_map/ppermute | solution.py:22
  128.2 1.3 collective-permute-start.19
  129.5 3.1 %collective-permute-done.19 = f32[6,1,256]{2,1,0:T(1,128)S(1)} collective-permute-done((f32[6,1,256]{2,1,0:T(1,128)S(1)}, f32[6,1,256]{2,1,0:T(1,128)S(1)}, u32[]{:S(2)}, u32[]{:S(2)}) %collective-permute-start.19) | collective-permute-done | bytes 6176 | tf_op jit(solution)/shard_map/ppermute | solution.py:24
  132.6 0.3 select_maximum_fusion
  133.1 0.9 fusion.26
  (66 shorter events, 1.6 us)
Async XLA Ops:
  1.9 21.7 %collective-permute-start = (f32[1,32,256]{2,1,0:T(8,128)S(1)}, f32[1,32,256]{2,1,0:T(8,128)S(1)}, u32[]{:S(2)}, u32[]{:S(2)}) collective-permute-start(f32[1,32,256]{2,1,0:T(8,128)S(1)} %get-tuple-element.37), channel_id=1, source_target_pairs={{0,2},{2,4},{4,6},{6,8},{8,10},{10,12},{12,14},{14,16},{16,18},{18... | collective-permute-start | bytes 98312 | tf_op jit(solution)/shard_map/ppermute | solution.py:22
  6.4 17.2 %collective-permute-start.1 = (f32[1,32,256]{2,1,0:T(8,128)S(1)}, f32[1,32,256]{2,1,0:T(8,128)S(1)}, u32[]{:S(2)}, u32[]{:S(2)}) collective-permute-start(f32[1,32,256]{2,1,0:T(8,128)S(1)} %get-tuple-element.38), channel_id=1, source_target_pairs={{2,0},{4,2},{6,4},{8,6},{10,8},{12,10},{14,12},{16,14},{18,16},{20... | collective-permute-start | bytes 98312 | tf_op jit(solution)/shard_map/ppermute | solution.py:24
  8.4 13.9 %copy-start.1 = (s32[1,2]{1,0:T(1,128)S(1)}, s32[1,2]{1,0:T(1,128)}, u32[]{:S(2)}) copy-start(s32[1,2]{1,0:T(1,128)} %param.7) | copy-start | bytes 28
  8.4 23.9 %copy-start = (f32[4,32,256]{2,1,0:T(8,128)S(1)}, f32[4,32,256]{2,1,0:T(8,128)}, u32[]{:S(2)}) copy-start(f32[4,32,256]{2,1,0:T(8,128)} %param.4) | copy-start | bytes 393220
  23.7 8.3 %collective-permute-start.2 = (f32[6,1,256]{2,1,0:T(1,128)S(1)}, f32[6,1,256]{2,1,0:T(1,128)S(1)}, u32[]{:S(2)}, u32[]{:S(2)}) collective-permute-start(f32[6,1,256]{2,1,0:T(1,128)S(1)} %get-tuple-element.27), channel_id=1, source_target_pairs={{0,1},{2,3},{4,5},{6,7},{8,9},{10,11},{12,13},{14,15},{16,17},{18,... | collective-permute-start | bytes 18440 | tf_op jit(solution)/shard_map/ppermute | solution.py:22
  26.8 5.2 %collective-permute-start.3 = (f32[6,1,256]{2,1,0:T(1,128)S(1)}, f32[6,1,256]{2,1,0:T(1,128)S(1)}, u32[]{:S(2)}, u32[]{:S(2)}) collective-permute-start(f32[6,1,256]{2,1,0:T(1,128)S(1)} %get-tuple-element.28), channel_id=1, source_target_pairs={{1,0},{3,2},{5,4},{7,6},{9,8},{11,10},{13,12},{15,14},{17,16},{19,... | collective-permute-start | bytes 18440 | tf_op jit(solution)/shard_map/ppermute | solution.py:24
  32.4 7.1 %collective-permute-start.4 = (f32[1,32,256]{2,1,0:T(8,128)S(1)}, f32[1,32,256]{2,1,0:T(8,128)S(1)}, u32[]{:S(2)}, u32[]{:S(2)}) collective-permute-start(f32[1,32,256]{2,1,0:T(8,128)S(1)} %get-tuple-element.35), channel_id=1, source_target_pairs={{0,2},{2,4},{4,6},{6,8},{8,10},{10,12},{12,14},{14,16},{16,18},{18... | collective-permute-start | bytes 98312 | tf_op jit(solution)/shard_map/ppermute | solution.py:22
  37.5 5.2 %collective-permute-start.5 = (f32[1,32,256]{2,1,0:T(8,128)S(1)}, f32[1,32,256]{2,1,0:T(8,128)S(1)}, u32[]{:S(2)}, u32[]{:S(2)}) collective-permute-start(f32[1,32,256]{2,1,0:T(8,128)S(1)} %get-tuple-element.36), channel_id=1, source_target_pairs={{2,0},{4,2},{6,4},{8,6},{10,8},{12,10},{14,12},{16,14},{18,16},{20... | collective-permute-start | bytes 98312 | tf_op jit(solution)/shard_map/ppermute | solution.py:24
  42.8 5.2 %collective-permute-start.6 = (f32[6,1,256]{2,1,0:T(1,128)S(1)}, f32[6,1,256]{2,1,0:T(1,128)S(1)}, u32[]{:S(2)}, u32[]{:S(2)}) collective-permute-start(f32[6,1,256]{2,1,0:T(1,128)S(1)} %get-tuple-element.25), channel_id=1, source_target_pairs={{0,1},{2,3},{4,5},{6,7},{8,9},{10,11},{12,13},{14,15},{16,17},{18,... | collective-permute-start | bytes 18440 | tf_op jit(solution)/shard_map/ppermute | solution.py:22
  46.5 4.4 %collective-permute-start.7 = (f32[6,1,256]{2,1,0:T(1,128)S(1)}, f32[6,1,256]{2,1,0:T(1,128)S(1)}, u32[]{:S(2)}, u32[]{:S(2)}) collective-permute-start(f32[6,1,256]{2,1,0:T(1,128)S(1)} %get-tuple-element.26), channel_id=1, source_target_pairs={{1,0},{3,2},{5,4},{7,6},{9,8},{11,10},{13,12},{15,14},{17,16},{19,... | collective-permute-start | bytes 18440 | tf_op jit(solution)/shard_map/ppermute | solution.py:24
  51.7 5.3 %collective-permute-start.8 = (f32[1,32,256]{2,1,0:T(8,128)S(1)}, f32[1,32,256]{2,1,0:T(8,128)S(1)}, u32[]{:S(2)}, u32[]{:S(2)}) collective-permute-start(f32[1,32,256]{2,1,0:T(8,128)S(1)} %get-tuple-element.33), channel_id=1, source_target_pairs={{0,2},{2,4},{4,6},{6,8},{8,10},{10,12},{12,14},{14,16},{16,18},{18... | collective-permute-start | bytes 98312 | tf_op jit(solution)/shard_map/ppermute | solution.py:22
  55.0 5.5 %collective-permute-start.9 = (f32[1,32,256]{2,1,0:T(8,128)S(1)}, f32[1,32,256]{2,1,0:T(8,128)S(1)}, u32[]{:S(2)}, u32[]{:S(2)}) collective-permute-start(f32[1,32,256]{2,1,0:T(8,128)S(1)} %get-tuple-element.34), channel_id=1, source_target_pairs={{2,0},{4,2},{6,4},{8,6},{10,8},{12,10},{14,12},{16,14},{18,16},{20... | collective-permute-start | bytes 98312 | tf_op jit(solution)/shard_map/ppermute | solution.py:24
  60.5 3.0 %collective-permute-start.10 = (f32[6,1,256]{2,1,0:T(1,128)S(1)}, f32[6,1,256]{2,1,0:T(1,128)S(1)}, u32[]{:S(2)}, u32[]{:S(2)}) collective-permute-start(f32[6,1,256]{2,1,0:T(1,128)S(1)} %get-tuple-element.23), channel_id=1, source_target_pairs={{0,1},{2,3},{4,5},{6,7},{8,9},{10,11},{12,13},{14,15},{16,17},{18,... | collective-permute-start | bytes 18440 | tf_op jit(solution)/shard_map/ppermute | solution.py:22
  62.2 4.4 %collective-permute-start.11 = (f32[6,1,256]{2,1,0:T(1,128)S(1)}, f32[6,1,256]{2,1,0:T(1,128)S(1)}, u32[]{:S(2)}, u32[]{:S(2)}) collective-permute-start(f32[6,1,256]{2,1,0:T(1,128)S(1)} %get-tuple-element.24), channel_id=1, source_target_pairs={{1,0},{3,2},{5,4},{7,6},{9,8},{11,10},{13,12},{15,14},{17,16},{19,... | collective-permute-start | bytes 18440 | tf_op jit(solution)/shard_map/ppermute | solution.py:24
  99.9 6.7 %collective-permute-start.12 = (f32[1,32,256]{2,1,0:T(8,128)S(1)}, f32[1,32,256]{2,1,0:T(8,128)S(1)}, u32[]{:S(2)}, u32[]{:S(2)}) collective-permute-start(f32[1,32,256]{2,1,0:T(8,128)S(1)} %get-tuple-element.31), channel_id=1, source_target_pairs={{0,2},{2,4},{4,6},{6,8},{8,10},{10,12},{12,14},{14,16},{16,18},{18... | collective-permute-start | bytes 98312 | tf_op jit(solution)/shard_map/ppermute | solution.py:22
  104.6 5.2 %collective-permute-start.13 = (f32[1,32,256]{2,1,0:T(8,128)S(1)}, f32[1,32,256]{2,1,0:T(8,128)S(1)}, u32[]{:S(2)}, u32[]{:S(2)}) collective-permute-start(f32[1,32,256]{2,1,0:T(8,128)S(1)} %get-tuple-element.32), channel_id=1, source_target_pairs={{2,0},{4,2},{6,4},{8,6},{10,8},{12,10},{14,12},{16,14},{18,16},{20... | collective-permute-start | bytes 98312 | tf_op jit(solution)/shard_map/ppermute | solution.py:24
  109.9 2.9 %collective-permute-start.14 = (f32[6,1,256]{2,1,0:T(1,128)S(1)}, f32[6,1,256]{2,1,0:T(1,128)S(1)}, u32[]{:S(2)}, u32[]{:S(2)}) collective-permute-start(f32[6,1,256]{2,1,0:T(1,128)S(1)} %get-tuple-element.21), channel_id=1, source_target_pairs={{0,1},{2,3},{4,5},{6,7},{8,9},{10,11},{12,13},{14,15},{16,17},{18,... | collective-permute-start | bytes 18440 | tf_op jit(solution)/shard_map/ppermute | solution.py:22
  111.5 4.4 %collective-permute-start.15 = (f32[6,1,256]{2,1,0:T(1,128)S(1)}, f32[6,1,256]{2,1,0:T(1,128)S(1)}, u32[]{:S(2)}, u32[]{:S(2)}) collective-permute-start(f32[6,1,256]{2,1,0:T(1,128)S(1)} %get-tuple-element.22), channel_id=1, source_target_pairs={{1,0},{3,2},{5,4},{7,6},{9,8},{11,10},{13,12},{15,14},{17,16},{19,... | collective-permute-start | bytes 18440 | tf_op jit(solution)/shard_map/ppermute | solution.py:24
  116.7 6.2 %collective-permute-start.16 = (f32[1,32,256]{2,1,0:T(8,128)S(1)}, f32[1,32,256]{2,1,0:T(8,128)S(1)}, u32[]{:S(2)}, u32[]{:S(2)}) collective-permute-start(f32[1,32,256]{2,1,0:T(8,128)S(1)} %get-tuple-element.29), channel_id=1, source_target_pairs={{0,2},{2,4},{4,6},{6,8},{8,10},{10,12},{12,14},{14,16},{16,18},{18... | collective-permute-start | bytes 98312 | tf_op jit(solution)/shard_map/ppermute | solution.py:22
  120.9 5.6 %collective-permute-start.17 = (f32[1,32,256]{2,1,0:T(8,128)S(1)}, f32[1,32,256]{2,1,0:T(8,128)S(1)}, u32[]{:S(2)}, u32[]{:S(2)}) collective-permute-start(f32[1,32,256]{2,1,0:T(8,128)S(1)} %get-tuple-element.30), channel_id=1, source_target_pairs={{2,0},{4,2},{6,4},{8,6},{10,8},{12,10},{14,12},{16,14},{18,16},{20... | collective-permute-start | bytes 98312 | tf_op jit(solution)/shard_map/ppermute | solution.py:24
  126.5 3.0 %collective-permute-start.18 = (f32[6,1,256]{2,1,0:T(1,128)S(1)}, f32[6,1,256]{2,1,0:T(1,128)S(1)}, u32[]{:S(2)}, u32[]{:S(2)}) collective-permute-start(f32[6,1,256]{2,1,0:T(1,128)S(1)} %get-tuple-element.19), channel_id=1, source_target_pairs={{0,1},{2,3},{4,5},{6,7},{8,9},{10,11},{12,13},{14,15},{16,17},{18,... | collective-permute-start | bytes 18440 | tf_op jit(solution)/shard_map/ppermute | solution.py:22
  128.2 4.4 %collective-permute-start.19 = (f32[6,1,256]{2,1,0:T(1,128)S(1)}, f32[6,1,256]{2,1,0:T(1,128)S(1)}, u32[]{:S(2)}, u32[]{:S(2)}) collective-permute-start(f32[6,1,256]{2,1,0:T(1,128)S(1)} %get-tuple-element.20), channel_id=1, source_target_pairs={{1,0},{3,2},{5,4},{7,6},{9,8},{11,10},{13,12},{15,14},{17,16},{19,... | collective-permute-start | bytes 18440 | tf_op jit(solution)/shard_map/ppermute | solution.py:24
where the time goes:
time: 136 us; the launch traced here: 134 us
  starting transfers between devices  49.7 us (37%)
  local copies, waits for them, and re-layouts  31.3 us (23%)
  waiting for transfers between devices  25.7 us (19%)
  other arithmetic  18.2 us (13%)
  blocking collectives  7.12 us (5%)
  between operations  2.07 us (2%)
    ppermute x10, starting transfers between devices, extended(): lax.ppermute(tail, axis, [(i, (i + 1) % count) for i in range(ends)])  33.6 us
    ppermute x10, waiting for transfers between devices, extended(): lax.ppermute(head, axis, [((i + 1) % count, i) for i in range(ends)])  25.7 us
    reshape x2, local copies, waits for them, and re-layouts, coarsen(): values.reshape(size_x // 2, 2, size_y // 2, 2, size_z // 2, 2)  19.6 us
    ppermute x10, starting transfers between devices, extended(): lax.ppermute(head, axis, [((i + 1) % count, i) for i in range(ends)])  16.1 us
    reduce_sum x2, other arithmetic, coarsen(): values.reshape(size_x // 2, 2, size_y // 2, 2, size_z // 2, 2)  8.04 us
    reshape x1, local copies, waits for them, and re-layouts, on_device(): fine_corr = jnp.broadcast_to(correction[:, None, :, None, :, None], (size...  6.93 us
    all_gather x1, blocking collectives, on_device(): lax.all_gather(coarse_cond, 'gy', axis=1, tiled=True)  3.86 us
    broadcast_in_dim x1, local copies, waits for them, and re-layouts, on_device(): jnp.broadcast_to(correction[:, None, :, None, :, None], (size_x, 2, size_...  3.85 us
  transfers between devices with their start and end apart: 20, of which 8 were waited for; matrix products, arithmetic and copies ran while one was open for 12% of the time, Pallas kernels for 0%

commit v1 on v0

v1 whole, which is shorter than its diff:
```python
import functools

import jax
import jax.numpy as jnp
from jax import lax
from jax.experimental import pallas as pl
from jax.experimental.pallas import tpu as pltpu
from jax.sharding import PartitionSpec as P

POST_SWEEPS = 2
COARSE_SWEEPS = 6
RELAX_WEIGHT = 0.6
MASS_TERM = 0.1

MESH = pl.DeviceIdType.MESH
WIDE = 3
HALF = 4
COND, SOURCE, ITERATE = 0, 1, 2
WIDTHS = (3, 2, 2)
STEPS = ((-1, 0), (1, 0), (0, -1), (0, 1), (-1, -1), (1, -1), (-1, 1), (1, 1))


def kernel(
    n_gx, n_gy,
    owners_ref, table_ref, source_ref, region_ref, out_ref,
    ext, after, before, labels, weight, diag2, group, squeezed, whole_corr, spread,
    send_sem, recv_sem, g_send, g_recv, in_sem,
):
    nx, ny, nz = out_ref.shape
    cx, cy, cz = nx // 2, ny // 2, nz // 2
    first, last = WIDE, WIDE + nx
    gx, gy = lax.axis_index("gx"), lax.axis_index("gy")

    def exists(dx, dy):
        x, y = gx + dx, gy + dy
        return (x >= 0) & (x < n_gx) & (y >= 0) & (y < n_gy)

    load_source = pltpu.make_async_copy(
        source_ref, ext.at[SOURCE, pl.ds(first, nx), pl.ds(0, ny)], in_sem.at[0]
    )
    load_region = pltpu.make_async_copy(region_ref, labels, in_sem.at[1])
    load_region.start()
    load_source.start()

    barrier = pltpu.get_barrier_semaphore()
    count = jnp.int32(0)
    for dx, dy in STEPS:
        near = exists(dx, dy)

        @pl.when(near)
        def _():
            pl.semaphore_signal(
                barrier, inc=1, device_id=(gx + dx, gy + dy), device_id_type=MESH
            )

        count = count + near.astype(jnp.int32)
    for off in range(2 - n_gy - 1, n_gy):
        if abs(off) >= 2:
            near = exists(0, off)

            @pl.when(near)
            def _():
                pl.semaphore_signal(
                    barrier, inc=1, device_id=(gx, gy + off), device_id_type=MESH
                )

            count = count + near.astype(jnp.int32)

    def planes_in(dx, w):
        return {0: (first, nx), -1: (last, w), 1: (first - w, w)}[dx]

    def planes_out(dx, w):
        return {0: (first, nx), -1: (first, w), 1: (last - w, w)}[dx]

    def landing(kind, dx, dy, w):
        start, size = planes_in(dx, w)
        if dy == 0:
            return ext.at[kind, pl.ds(start, size), pl.ds(0, ny)]
        return (after if dy < 0 else before).at[kind, pl.ds(start, size)]

    def remote(kind, which):
        dx, dy = STEPS[which]
        w = WIDTHS[kind]
        start, size = planes_out(dx, w)
        rows = {0: pl.ds(0, ny), -1: pl.ds(0, 8), 1: pl.ds(ny - 8, 8)}[dy]
        return pltpu.make_async_remote_copy(
            src_ref=ext.at[kind, pl.ds(start, size), rows],
            dst_ref=landing(kind, dx, dy, w),
            send_sem=send_sem.at[kind, which],
            recv_sem=recv_sem.at[kind, which],
            device_id=(gx + dx, gy + dy),
            device_id_type=MESH,
        )

    def send(kind):
        for which, (dx, dy) in enumerate(STEPS):
            @pl.when(exists(dx, dy))
            def _():
                remote(kind, which).start()

    def receive(kind):
        for which, (dx, dy) in enumerate(STEPS):
            @pl.when(exists(-dx, -dy))
            def _():
                remote(kind, which).wait_recv()

    def finish(kind):
        for which, (dx, dy) in enumerate(STEPS):
            @pl.when(exists(dx, dy))
            def _():
                remote(kind, which).wait_send()

    for dx, dy in STEPS:
        @pl.when(jnp.logical_not(exists(-dx, -dy)))
        def _():
            for kind in range(3):
                ref = landing(kind, dx, dy, WIDTHS[kind])
                ref[...] = jnp.zeros(ref.shape, jnp.float32)

    row8 = lax.broadcasted_iota(jnp.int32, (8, nz), 0)

    def join(kind):
        w = WIDTHS[kind]
        for i in range(first - w, last + w):
            ext[kind, i, pl.ds(ny, 8), :] = jnp.where(
                row8 < HALF, after[kind, i], before[kind, i]
            )

    load_region.wait()
    pair = jnp.concatenate([table_ref[...], table_ref[...]], axis=1)
    table = jnp.broadcast_to(pair, (8, 128))
    for i in range(nx):
        for r in range(0, ny, 8):
            for c in range(0, nz, 128):
                spot = labels[i, pl.ds(r, 8), pl.ds(c, 128)]
                ext[COND, first + i, pl.ds(r, 8), pl.ds(c, 128)] = jnp.take_along_axis(
                    table, spot, axis=1
                )

    pl.semaphore_wait(barrier, count)
    send(COND)
    load_source.wait()
    send(SOURCE)

    lane = lax.broadcasted_iota(jnp.int32, (1, nz), 1)
    z_low = jnp.where(lane == 0, 0.0, 0.5)
    z_high = jnp.where(lane == nz - 1, 0.0, 0.5)
    rows = ny + 8

    def blend(a, b, c):
        u = b + 0.5 * (a + c)
        u = u + 0.5 * (pltpu.roll(u, 1, 0) + pltpu.roll(u, rows - 1, 0))
        return u + z_low * pltpu.roll(u, 1, 1) + z_high * pltpu.roll(u, nz - 1, 1)

    lane128 = lax.broadcasted_iota(jnp.int32, (8, 128), 1)
    even = lax.rem(2 * lane128, jnp.int32(128))
    half_of = lane128 // 2

    def coarsen(pairs, kind):
        for i, pair_sum in enumerate(pairs):
            total = pair_sum + pltpu.roll(pair_sum, nz - 1, 1)
            for r in range(0, ny, 8):
                low = jnp.take_along_axis(total[r:r + 8, :128], even, axis=1)
                high = jnp.take_along_axis(total[r:r + 8, 128:], even, axis=1)
                squeezed[i, pl.ds(r, 8), :] = jnp.where(lane128 < 64, low, high)
            block = squeezed[i, pl.ds(0, cy, stride=2), :] + squeezed[i, pl.ds(1, cy, stride=2), :]
            group[kind, i, pl.ds(pl.multiple_of(gy * cy, 8), cy), :] = 0.125 * block

    def gather(kind, off):
        mine = group.at[kind, :, pl.ds(pl.multiple_of(gy * cy, 8), cy)]
        return pltpu.make_async_remote_copy(
            src_ref=mine,
            dst_ref=mine,
            send_sem=g_send.at[kind, off - 1],
            recv_sem=g_recv.at[kind, off - 1],
            device_id=(gx, lax.rem(gy + off, n_gy)),
            device_id_type=MESH,
        )

    def gather_in(kind, off):
        sender = lax.rem(gy + n_gy - off, n_gy)
        theirs = group.at[kind, :, pl.ds(pl.multiple_of(sender * cy, 8), cy)]
        return pltpu.make_async_remote_copy(
            src_ref=theirs,
            dst_ref=theirs,
            send_sem=g_send.at[kind, off - 1],
            recv_sem=g_recv.at[kind, off - 1],
            device_id=(gx, sender),
            device_id_type=MESH,
        )

    coarsen(
        [ext[COND, first + 2 * i, pl.ds(0, ny), :] + ext[COND, first + 2 * i + 1, pl.ds(0, ny), :]
         for i in range(cx)],
        0,
    )
    for off in range(1, n_gy):
        gather(0, off).start()

    receive(COND)
    join(COND)
    row = lax.broadcasted_iota(jnp.int32, (rows, 1), 0)
    y = gy * ny + jnp.where(row < ny + HALF, row, row - rows)
    in_y = jnp.where((y >= 0) & (y < n_gy * ny), RELAX_WEIGHT, 0.0)
    for i in range(first - 2, last + 2):
        cond = ext[COND, i]
        mixed = blend(ext[COND, i - 1], cond, ext[COND, i + 1])
        x = gx * nx + (i - first)
        in_x = jnp.where((x >= 0) & (x < n_gx * nx), 1.0, 0.0)
        weight[i] = (in_y * in_x) / (MASS_TERM + 6.0 * cond + mixed)
        diag2[i] = MASS_TERM + 8.0 * cond + mixed

    def defect(kind, i, values, flux):
        lhs = ext[COND, i] * blend(values[i - 1], values[i], values[i + 1])
        return ext[SOURCE, i] - diag2[i] * values[i] + lhs + blend(flux[i - 1], flux[i], flux[i + 1])

    receive(SOURCE)
    join(SOURCE)
    values, flux = {}, {}
    for i in range(first - 2, last + 2):
        values[i] = weight[i] * ext[SOURCE, i]
        flux[i] = ext[COND, i] * values[i]
    smooth = {}
    for i in range(first - 1, last + 1):
        smooth[i] = values[i] + weight[i] * defect(SOURCE, i, values, flux)
    flux = {i: ext[COND, i] * smooth[i] for i in smooth}
    pairs = []
    for i in range(cx):
        j = first + 2 * i
        pairs.append(
            defect(SOURCE, j, smooth, flux)[:ny] + defect(SOURCE, j + 1, smooth, flux)[:ny]
        )
    coarsen(pairs, 1)
    for off in range(1, n_gy):
        gather(1, off).start()
    for i in range(first, last):
        ext[ITERATE, i, pl.ds(0, ny), :] = smooth[i][:ny]

    all_y = n_gy * cy
    crow = lax.broadcasted_iota(jnp.int32, (all_y, cz), 0)
    clane = lax.broadcasted_iota(jnp.int32, (all_y, cz), 1)
    owner = jnp.full((all_y, cz), owners_ref[0, 0], jnp.int32)
    for c in range(1, n_gy):
        owner = jnp.where(crow >= c * cy, owners_ref[0, c], owner)
    mask = jnp.where(owner == owners_ref[0, gy], 1.0, 0.0)
    y_low = jnp.where(crow == 0, 0.0, 0.5)
    y_high = jnp.where(crow == all_y - 1, 0.0, 0.5)
    cz_low = jnp.where(clane == 0, 0.0, 0.5)
    cz_high = jnp.where(clane == cz - 1, 0.0, 0.5)

    def coarse_blend(planes):
        mixed = []
        for i, u in enumerate(planes):
            if i > 0:
                u = u + 0.5 * planes[i - 1]
            if i + 1 < cx:
                u = u + 0.5 * planes[i + 1]
            u = u + y_low * pltpu.roll(u, 1, 0) + y_high * pltpu.roll(u, all_y - 1, 0)
            mixed.append(u + cz_low * pltpu.roll(u, 1, 1) + cz_high * pltpu.roll(u, cz - 1, 1))
        return mixed

    for off in range(1, n_gy):
        gather_in(0, off).wait_recv()
    cond_c = [mask * group[0, i] for i in range(cx)]
    mixed = coarse_blend(cond_c)
    diag_c = [MASS_TERM + 1.5 * k + 0.25 * b for k, b in zip(cond_c, mixed)]
    weight_c = [RELAX_WEIGHT * mask / d for d in diag_c]
    diag_sum = jnp.sum(functools.reduce(jnp.add, [mask * d for d in diag_c]), keepdims=True)

    for off in range(1, n_gy):
        gather_in(1, off).wait_recv()
    res_c = [mask * group[1, i] for i in range(cx)]

    def coarse_defect(e):
        straight = coarse_blend(e)
        carried = coarse_blend([k * v for k, v in zip(cond_c, e)])
        return [
            res_c[i] - (diag_c[i] + 0.5 * cond_c[i]) * e[i]
            + 0.25 * (cond_c[i] * straight[i] + carried[i])
            for i in range(cx)
        ]

    e = [w * r for w, r in zip(weight_c, res_c)]
    for _ in range(COARSE_SWEEPS - 1):
        d = coarse_defect(e)
        e = [e[i] + weight_c[i] * d[i] for i in range(cx)]
    d = coarse_defect(e)
    left = jnp.sum(functools.reduce(jnp.add, [mask * v for v in d]), keepdims=True)
    ratio = left / jnp.maximum(diag_sum, 1.0)
    for i in range(cx):
        whole_corr[i] = e[i] + mask * ratio
        mine = whole_corr[i, pl.ds(pl.multiple_of(gy * cy, 8), cy), :]
        spread[i, pl.ds(0, cy, stride=2), :] = mine
        spread[i, pl.ds(1, cy, stride=2), :] = mine
    for i in range(cx):
        for r in range(0, ny, 8):
            tile = spread[i, pl.ds(r, 8), :]
            for part in range(2):
                wide = jnp.take_along_axis(tile, half_of + 64 * part, axis=1)
                for j in (first + 2 * i, first + 2 * i + 1):
                    at = (ITERATE, j, pl.ds(r, 8), pl.ds(128 * part, 128))
                    ext[at] = ext[at] + wide

    send(ITERATE)
    receive(ITERATE)
    join(ITERATE)
    values = {i: ext[ITERATE, i] for i in range(first - 2, last + 2)}
    for sweep in range(POST_SWEEPS):
        reach = POST_SWEEPS - 1 - sweep
        flux = {i: ext[COND, i] * values[i] for i in values}
        values = {
            i: values[i] + weight[i] * defect(ITERATE, i, values, flux)
            for i in range(first - reach, last + reach)
        }
    for i in range(nx):
        out_ref[i] = values[first + i][:ny]

    for kind in range(3):
        finish(kind)
    for kind in range(2):
        for off in range(1, n_gy):
            gather(kind, off).wait_send()


def on_device(source, region, permeability, owners, *, n_gx, n_gy):
    nx, ny, nz = source.shape
    planes = nx + 2 * WIDE
    f32 = jnp.float32
    return pl.pallas_call(
        functools.partial(kernel, n_gx, n_gy),
        out_shape=jax.ShapeDtypeStruct(source.shape, f32),
        in_specs=[
            pl.BlockSpec(memory_space=pltpu.SMEM),
            pl.BlockSpec(memory_space=pltpu.VMEM),
            pl.BlockSpec(memory_space=pl.ANY),
            pl.BlockSpec(memory_space=pl.ANY),
        ],
        out_specs=pl.BlockSpec(memory_space=pltpu.VMEM),
        scratch_shapes=[
            pltpu.VMEM((3, planes, ny + 8, nz), f32),
            pltpu.VMEM((3, planes, 8, nz), f32),
            pltpu.VMEM((3, planes, 8, nz), f32),
            pltpu.VMEM((nx, ny, nz), jnp.int32),
            pltpu.VMEM((planes, ny + 8, nz), f32),
            pltpu.VMEM((planes, ny + 8, nz), f32),
            pltpu.VMEM((2, nx // 2, n_gy * ny // 2, nz // 2), f32),
            pltpu.VMEM((nx // 2, ny, nz // 2), f32),
            pltpu.VMEM((nx // 2, n_gy * ny // 2, nz // 2), f32),
            pltpu.VMEM((nx // 2, ny, nz // 2), f32),
            pltpu.SemaphoreType.DMA((3, 8)),
            pltpu.SemaphoreType.DMA((3, 8)),
            pltpu.SemaphoreType.DMA((2, n_gy - 1)),
            pltpu.SemaphoreType.DMA((2, n_gy - 1)),
            pltpu.SemaphoreType.DMA((2,)),
        ],
        compiler_params=pltpu.CompilerParams(
            collective_id=0, has_side_effects=True, vmem_limit_bytes=16 * 1024 * 1024
        ),
    )(owners, permeability[None, :], source, region)


def solution(mesh):
    placed = (P("gx", "gy", None), P("gx", "gy", None), P(), P("gx", None))
    body = functools.partial(on_device, n_gx=mesh.shape["gx"], n_gy=mesh.shape["gy"])
    return jax.shard_map(
        body, mesh=mesh, in_specs=placed, out_specs=P("gx", "gy", None), check_vma=False
    )
```

time: 136 us -> 22.8 us (0.17); the launches traced: 134 us -> 22.6 us
  starting transfers between devices: 49.7 us -> 0 us
  local copies, waits for them, and re-layouts: 31.3 us -> 3.13 us
  waiting for transfers between devices: 25.7 us -> 0 us
  Pallas kernels: 0 us -> 19.5 us
  other arithmetic: 18.2 us -> 0 us
  blocking collectives: 7.12 us -> 0 us
  between operations: 2.07 us -> 0.01 us
    ppermute x20 -> x0, starting transfers between devices: 49.7 us -> none  [the longest x10 33.6 us: extended(): lax.ppermute(tail, axis, [(i, (i + 1) % count) for i in range(ends)])]
    reshape x3 -> x0, local copies, waits for them, and re-layouts: 26.5 us -> none  [the longest x2 19.6 us: coarsen(): values.reshape(size_x // 2, 2, size_y // 2, 2, size_z // 2, 2)]
    ppermute x20 -> x0, waiting for transfers between devices: 25.7 us -> none  [the longest x10 25.7 us: extended(): lax.ppermute(head, axis, [((i + 1) % count, i) for i in range(ends)])]
    pallas_call x0 -> x1, Pallas kernels: none -> 19.5 us  [on_device(): pl.pallas_call(functools.partial(kernel, n_gx, n_gy), out_shape=jax.Shape...]
    reduce_sum x4 -> x0, other arithmetic: 10.7 us -> none  [the longest x2 8.04 us: coarsen(): values.reshape(size_x // 2, 2, size_y // 2, 2, size_z // 2, 2)]
    all_gather x2 -> x0, blocking collectives: 7.12 us -> none  [the longest x1 3.86 us: on_device(): lax.all_gather(coarse_cond, 'gy', axis=1, tiled=True)]
    add x43 -> x0, other arithmetic: 4.02 us -> none  [the longest x15 1.69 us: stencil_sum(): blended = 0.5 * padded[:-2] + padded[1:-1] + 0.5 * padded[2:]]
    broadcast_in_dim x3 -> x0, local copies, waits for them, and re-layouts: 3.93 us -> none  [the longest x1 3.85 us: on_device(): jnp.broadcast_to(correction[:, None, :, None, :, None], (size_x, 2, size_...]
  transfers between devices with their start and end apart: 20 -> 0, of which waited for: 8 -> 0; matrix products, arithmetic and copies ran while one was open for 12% -> 0% of each run, Pallas kernels for 0% -> 0%
where the time goes in v1:
time: 22.8 us; the launch traced here: 22.6 us
  Pallas kernels  19.5 us (86%)
  local copies, waits for them, and re-layouts  3.13 us (14%)
    pallas_call x1, Pallas kernels, on_device(): pl.pallas_call(functools.partial(kernel, n_gx, n_gy), out_shape=jax.Shape...  19.5 us
    unnamed x9, local copies, waits for them, and re-layouts  3.13 us

profile of v1, /device:TPU:1, one launch (start us, length us, event | category | flops | bytes accessed | tf_op | source)
XLA Modules:
  0.0 22.6 jit_solution(7886444718418682507)
XLA Ops:
  0.0 0.0 copy-start.2
  0.0 0.0 copy-start.3
  0.0 0.7 %copy-done.2 = s32[1,2]{1,0:T(1,128)S(1)} copy-done((s32[1,2]{1,0:T(1,128)S(1)}, s32[1,2]{1,0:T(1,128)}, u32[]{:S(2)}) %copy-start.2) | copy-done | bytes 32
  0.7 0.0 copy-done.3
  0.7 0.0 copy-start
  0.7 0.9 %copy-done = f32[4,32,256]{2,1,0:T(8,128)S(1)} copy-done((f32[4,32,256]{2,1,0:T(8,128)S(1)}, f32[4,32,256]{2,1,0:T(8,128)}, u32[]{:S(2)}) %copy-start) | copy-done | bytes 131096
  1.6 0.0 copy-start.1
  1.6 0.9 %copy-done.1 = s32[4,32,256]{2,1,0:T(8,128)S(1)} copy-done((s32[4,32,256]{2,1,0:T(8,128)S(1)}, s32[4,32,256]{2,1,0:T(8,128)}, u32[]{:S(2)}) %copy-start.1) | copy-done | bytes 131096
  2.5 19.5 %shard_map.46 = f32[4,32,256]{2,1,0:T(8,128)S(1)} custom-call(s32[1,2]{1,0:T(1,128)S(1)} %copy-done.2, f32[1,64]{1,0:T(1,128)S(1)} %bitcast.1, f32[4,32,256]{2,1,0:T(8,128)S(1)} %copy-done, s32[4,32,256]{2,1,0:T(8,128)S(1)} %copy-done.1), custom_call_target="tpu_custom_call" | custom-call | tf_op jit(solution)/shard_map/pallas_call | solution.py:329
  21.9 0.7 %copy.6 = f32[4,32,256]{2,1,0:T(8,128)} copy(f32[4,32,256]{2,1,0:T(8,128)S(1)} %shard_map.46) | data formatting | bytes 262144
Async XLA Ops:
  0.0 0.7 %copy-start.2 = (s32[1,2]{1,0:T(1,128)S(1)}, s32[1,2]{1,0:T(1,128)}, u32[]{:S(2)}) copy-start(s32[1,2]{1,0:T(1,128)} %owners_ref.1) | copy-start | bytes 28
  0.0 0.7 %copy-start.3 = (f32[64]{0:T(128)S(1)}, f32[64]{0:T(128)}, u32[]{:S(2)}) copy-start(f32[64]{0:T(128)} %param.6) | copy-start | bytes 772
  0.7 0.9 %copy-start = (f32[4,32,256]{2,1,0:T(8,128)S(1)}, f32[4,32,256]{2,1,0:T(8,128)}, u32[]{:S(2)}) copy-start(f32[4,32,256]{2,1,0:T(8,128)} %source_ref.1) | copy-start | bytes 393220
  1.6 0.9 %copy-start.1 = (s32[4,32,256]{2,1,0:T(8,128)S(1)}, s32[4,32,256]{2,1,0:T(8,128)}, u32[]{:S(2)}) copy-start(s32[4,32,256]{2,1,0:T(8,128)} %region_ref.1) | copy-start | bytes 393220

commit v2 on v1

--- a/solution.py
+++ b/solution.py
@@ -22,9 +22,9 @@
 
 def kernel(
     n_gx, n_gy,
-    owners_ref, table_ref, source_ref, region_ref, out_ref,
-    ext, after, before, labels, weight, diag2, group, squeezed, whole_corr, spread,
-    send_sem, recv_sem, g_send, g_recv, in_sem,
+    owners_in, table_in, source_ref, region_ref, out_ref,
+    owners_ref, table_ref, ext, after, before, labels, weight, diag2, result, group, squeezed, whole_corr, spread,
+    send_sem, recv_sem, g_send, g_recv, in_sem, out_sem,
 ):
     nx, ny, nz = out_ref.shape
     cx, cy, cz = nx // 2, ny // 2, nz // 2
@@ -39,8 +39,12 @@
         source_ref, ext.at[SOURCE, pl.ds(first, nx), pl.ds(0, ny)], in_sem.at[0]
     )
     load_region = pltpu.make_async_copy(region_ref, labels, in_sem.at[1])
+    load_table = pltpu.make_async_copy(table_in, table_ref, in_sem.at[2])
+    load_owners = pltpu.make_async_copy(owners_in, owners_ref, in_sem.at[3])
     load_region.start()
+    load_table.start()
     load_source.start()
+    load_owners.start()
 
     barrier = pltpu.get_barrier_semaphore()
     count = jnp.int32(0)
@@ -126,6 +130,7 @@
                 row8 < HALF, after[kind, i], before[kind, i]
             )
 
+    load_table.wait()
     load_region.wait()
     pair = jnp.concatenate([table_ref[...], table_ref[...]], axis=1)
     table = jnp.broadcast_to(pair, (8, 128))
@@ -141,6 +146,7 @@
     send(COND)
     load_source.wait()
     send(SOURCE)
+    load_owners.wait()
 
     lane = lax.broadcasted_iota(jnp.int32, (1, nz), 1)
     z_low = jnp.where(lane == 0, 0.0, 0.5)
@@ -312,14 +318,19 @@
             i: values[i] + weight[i] * defect(ITERATE, i, values, flux)
             for i in range(first - reach, last + reach)
         }
+    stores = []
     for i in range(nx):
-        out_ref[i] = values[first + i][:ny]
+        result[i] = values[first + i][:ny]
+        stores.append(pltpu.make_async_copy(result.at[i], out_ref.at[i], out_sem.at[i]))
+        stores[i].start()
 
     for kind in range(3):
         finish(kind)
     for kind in range(2):
         for off in range(1, n_gy):
             gather(kind, off).wait_send()
+    for store in stores:
+        store.wait()
 
 
 def on_device(source, region, permeability, owners, *, n_gx, n_gy):
@@ -330,19 +341,22 @@
         functools.partial(kernel, n_gx, n_gy),
         out_shape=jax.ShapeDtypeStruct(source.shape, f32),
         in_specs=[
-            pl.BlockSpec(memory_space=pltpu.SMEM),
-            pl.BlockSpec(memory_space=pltpu.VMEM),
-            pl.BlockSpec(memory_space=pl.ANY),
-            pl.BlockSpec(memory_space=pl.ANY),
+            pl.BlockSpec(memory_space=pltpu.HBM),
+            pl.BlockSpec(memory_space=pltpu.HBM),
+            pl.BlockSpec(memory_space=pltpu.HBM),
+            pl.BlockSpec(memory_space=pltpu.HBM),
         ],
-        out_specs=pl.BlockSpec(memory_space=pltpu.VMEM),
+        out_specs=pl.BlockSpec(memory_space=pltpu.HBM),
         scratch_shapes=[
+            pltpu.SMEM((1, n_gy), jnp.int32),
+            pltpu.VMEM((1, permeability.shape[0]), f32),
             pltpu.VMEM((3, planes, ny + 8, nz), f32),
             pltpu.VMEM((3, planes, 8, nz), f32),
             pltpu.VMEM((3, planes, 8, nz), f32),
             pltpu.VMEM((nx, ny, nz), jnp.int32),
             pltpu.VMEM((planes, ny + 8, nz), f32),
             pltpu.VMEM((planes, ny + 8, nz), f32),
+            pltpu.VMEM((nx, ny, nz), f32),
             pltpu.VMEM((2, nx // 2, n_gy * ny // 2, nz // 2), f32),
             pltpu.VMEM((nx // 2, ny, nz // 2), f32),
             pltpu.VMEM((nx // 2, n_gy * ny // 2, nz // 2), f32),
@@ -351,10 +365,11 @@
             pltpu.SemaphoreType.DMA((3, 8)),
             pltpu.SemaphoreType.DMA((2, n_gy - 1)),
             pltpu.SemaphoreType.DMA((2, n_gy - 1)),
-            pltpu.SemaphoreType.DMA((2,)),
+            pltpu.SemaphoreType.DMA((4,)),
+            pltpu.SemaphoreType.DMA((nx,)),
         ],
         compiler_params=pltpu.CompilerParams(
-            collective_id=0, has_side_effects=True, vmem_limit_bytes=16 * 1024 * 1024
+            collective_id=0, has_side_effects=True, vmem_limit_bytes=60 * 1024 * 1024
         ),
     )(owners, permeability[None, :], source, region)
 

time: 22.8 us -> 21 us (0.921)
  local copies, waits for them, and re-layouts: 3.13 us -> 1.57 us
    unnamed x9 -> x1, local copies, waits for them, and re-layouts: 3.13 us -> 1.57 us
where the time goes in v2:
time: 21 us; the launch traced here: 20.9 us
  Pallas kernels  19.3 us (92%)
  local copies, waits for them, and re-layouts  1.57 us (7%)
    pallas_call x1, Pallas kernels, on_device(): pl.pallas_call(functools.partial(kernel, n_gx, n_gy), out_shape=jax.Shape...  19.3 us
    unnamed x1, local copies, waits for them, and re-layouts  1.57 us

profile of v2, /device:TPU:1, one launch (start us, length us, event | category | flops | bytes accessed | tf_op | source)
XLA Modules:
  0.0 20.9 jit_solution(8888316166902967490)
XLA Ops:
  0.0 19.3 %shard_map.46 = f32[4,32,256]{2,1,0:T(8,128)} custom-call(s32[1,2]{1,0:T(1,128)} %owners_in.1, f32[1,64]{1,0:T(1,128)} %bitcast.1, f32[4,32,256]{2,1,0:T(8,128)} %source_ref.1, s32[4,32,256]{2,1,0:T(8,128)} %region_ref.1), custom_call_target="tpu_custom_call" | custom-call | tf_op jit(solution)/shard_map/pallas_call | solution.py:340
  19.3 1.6 %copy.6 = f32[4,32,256]{2,1,0:T(8,128)} copy(f32[4,32,256]{2,1,0:T(8,128)} %shard_map.46) | data formatting | bytes 262144

commit v3 on v2

--- a/solution.py
+++ b/solution.py
@@ -23,7 +23,7 @@
 def kernel(
     n_gx, n_gy,
     owners_in, table_in, source_ref, region_ref, out_ref,
-    owners_ref, table_ref, ext, after, before, labels, weight, diag2, result, group, squeezed, whole_corr, spread,
+    owners_ref, table_ref, ext, packed, after, before, labels, weight, diag2, result, group, squeezed, whole_corr, spread,
     send_sem, recv_sem, g_send, g_recv, in_sem, out_sem,
 ):
     nx, ny, nz = out_ref.shape
@@ -80,15 +80,21 @@
         start, size = planes_in(dx, w)
         if dy == 0:
             return ext.at[kind, pl.ds(start, size), pl.ds(0, ny)]
+        start, size = {0: (2, cx), -1: (2 + cx, (w + 1) // 2), 1: (2 - (w + 1) // 2, (w + 1) // 2)}[dx]
         return (after if dy < 0 else before).at[kind, pl.ds(start, size)]
 
     def remote(kind, which):
         dx, dy = STEPS[which]
         w = WIDTHS[kind]
         start, size = planes_out(dx, w)
-        rows = {0: pl.ds(0, ny), -1: pl.ds(0, 8), 1: pl.ds(ny - 8, 8)}[dy]
+        if dy == 0:
+            source = ext.at[kind, pl.ds(start, size), pl.ds(0, ny)]
+        else:
+            tiles = (w + 1) // 2
+            start, size = {0: (0, cx), -1: (0, tiles), 1: (cx - tiles, tiles)}[dx]
+            source = packed.at[kind, max(dy, 0), pl.ds(start, size)]
         return pltpu.make_async_remote_copy(
-            src_ref=ext.at[kind, pl.ds(start, size), rows],
+            src_ref=source,
             dst_ref=landing(kind, dx, dy, w),
             send_sem=send_sem.at[kind, which],
             recv_sem=recv_sem.at[kind, which],
@@ -123,12 +129,28 @@
 
     row8 = lax.broadcasted_iota(jnp.int32, (8, nz), 0)
 
+    def pack(kind):
+        for s in range(cx):
+            a, b = first + 2 * s, first + 2 * s + 1
+            packed[kind, 0, s] = jnp.where(
+                row8 < HALF, ext[kind, a, pl.ds(0, 8), :],
+                pltpu.roll(ext[kind, b, pl.ds(0, 8), :], HALF, 0),
+            )
+            packed[kind, 1, s] = jnp.where(
+                row8 < HALF, pltpu.roll(ext[kind, a, pl.ds(ny - 8, 8), :], HALF, 0),
+                ext[kind, b, pl.ds(ny - 8, 8), :],
+            )
+
     def join(kind):
         w = WIDTHS[kind]
         for i in range(first - w, last + w):
-            ext[kind, i, pl.ds(ny, 8), :] = jnp.where(
-                row8 < HALF, after[kind, i], before[kind, i]
-            )
+            s, odd = divmod(i - first + 4, 2)
+            low, high = after[kind, s], before[kind, s]
+            if odd:
+                low = pltpu.roll(low, HALF, 0)
+            else:
+                high = pltpu.roll(high, HALF, 0)
+            ext[kind, i, pl.ds(ny, 8), :] = jnp.where(row8 < HALF, low, high)
 
     load_table.wait()
     load_region.wait()
@@ -142,9 +164,11 @@
                     table, spot, axis=1
                 )
 
+    pack(COND)
     pl.semaphore_wait(barrier, count)
     send(COND)
     load_source.wait()
+    pack(SOURCE)
     send(SOURCE)
     load_owners.wait()
 
@@ -307,6 +331,7 @@
                     at = (ITERATE, j, pl.ds(r, 8), pl.ds(128 * part, 128))
                     ext[at] = ext[at] + wide
 
+    pack(ITERATE)
     send(ITERATE)
     receive(ITERATE)
     join(ITERATE)
@@ -351,8 +376,9 @@
             pltpu.SMEM((1, n_gy), jnp.int32),
             pltpu.VMEM((1, permeability.shape[0]), f32),
             pltpu.VMEM((3, planes, ny + 8, nz), f32),
-            pltpu.VMEM((3, planes, 8, nz), f32),
-            pltpu.VMEM((3, planes, 8, nz), f32),
+            pltpu.VMEM((3, 2, nx // 2, 8, nz), f32),
+            pltpu.VMEM((3, nx // 2 + 4, 8, nz), f32),
+            pltpu.VMEM((3, nx // 2 + 4, 8, nz), f32),
             pltpu.VMEM((nx, ny, nz), jnp.int32),
             pltpu.VMEM((planes, ny + 8, nz), f32),
             pltpu.VMEM((planes, ny + 8, nz), f32),

time: 21 us -> 20.4 us (0.971)
  Pallas kernels: 19.3 us -> 18.7 us
    pallas_call x1, Pallas kernels: 19.3 us -> 18.7 us  [on_device(): pl.pallas_call(functools.partial(kernel, n_gx, n_gy), out_shape=jax.Shape...]
where the time goes in v3:
time: 20.4 us; the launch traced here: 20.2 us
  Pallas kernels  18.7 us (92%)
  local copies, waits for them, and re-layouts  1.57 us (8%)
    pallas_call x1, Pallas kernels, on_device(): pl.pallas_call(functools.partial(kernel, n_gx, n_gy), out_shape=jax.Shape...  18.7 us
    unnamed x1, local copies, waits for them, and re-layouts  1.57 us

profile of v3, /device:TPU:1, one launch (start us, length us, event | category | flops | bytes accessed | tf_op | source)
XLA Modules:
  0.0 20.2 jit_solution(11171197983222944395)
XLA Ops:
  0.0 18.7 %shard_map.46 = f32[4,32,256]{2,1,0:T(8,128)} custom-call(s32[1,2]{1,0:T(1,128)} %owners_in.1, f32[1,64]{1,0:T(1,128)} %bitcast.1, f32[4,32,256]{2,1,0:T(8,128)} %source_ref.1, s32[4,32,256]{2,1,0:T(8,128)} %region_ref.1), custom_call_target="tpu_custom_call" | custom-call | tf_op jit(solution)/shard_map/pallas_call | solution.py:365
  18.7 1.6 %copy.6 = f32[4,32,256]{2,1,0:T(8,128)} copy(f32[4,32,256]{2,1,0:T(8,128)} %shard_map.46) | data formatting | bytes 262144

commit v4 on v3

--- a/solution.py
+++ b/solution.py
@@ -23,8 +23,8 @@
 def kernel(
     n_gx, n_gy,
     owners_in, table_in, source_ref, region_ref, out_ref,
-    owners_ref, table_ref, ext, packed, after, before, labels, weight, diag2, result, group, squeezed, whole_corr, spread,
-    send_sem, recv_sem, g_send, g_recv, in_sem, out_sem,
+    owners_ref, table_ref, ext, packed, after, before, labels, weight, diag2, result, group, squeezed, whole_corr, spread, corr, corr_y, wide,
+    send_sem, recv_sem, g_send, g_recv, in_sem, out_sem, c_send, c_recv,
 ):
     nx, ny, nz = out_ref.shape
     cx, cy, cz = nx // 2, ny // 2, nz // 2
@@ -102,6 +102,23 @@
             device_id_type=MESH,
         )
 
+    def landing_corr(dx, dy):
+        at = {0: pl.ds(1, cx), -1: pl.ds(cx + 1, 1), 1: pl.ds(0, 1)}[dx]
+        return corr.at[at] if dy == 0 else corr_y.at[max(dy, 0), at]
+
+    def remote_corr(which):
+        dx, dy = STEPS[which]
+        at = {0: pl.ds(1, cx), -1: pl.ds(1, 1), 1: pl.ds(cx, 1)}[dx]
+        rows = {0: pl.ds(0, cy), -1: pl.ds(0, 8), 1: pl.ds(cy - 8, 8)}[dy]
+        return pltpu.make_async_remote_copy(
+            src_ref=corr.at[at, rows],
+            dst_ref=landing_corr(dx, dy),
+            send_sem=c_send.at[which],
+            recv_sem=c_recv.at[which],
+            device_id=(gx + dx, gy + dy),
+            device_id_type=MESH,
+        )
+
     def send(kind):
         for which, (dx, dy) in enumerate(STEPS):
             @pl.when(exists(dx, dy))
@@ -126,6 +143,8 @@
             for kind in range(3):
                 ref = landing(kind, dx, dy, WIDTHS[kind])
                 ref[...] = jnp.zeros(ref.shape, jnp.float32)
+            ref = landing_corr(dx, dy)
+            ref[...] = jnp.zeros(ref.shape, jnp.float32)
 
     row8 = lax.broadcasted_iota(jnp.int32, (8, nz), 0)
 
@@ -265,6 +284,8 @@
         gather(1, off).start()
     for i in range(first, last):
         ext[ITERATE, i, pl.ds(0, ny), :] = smooth[i][:ny]
+    pack(ITERATE)
+    send(ITERATE)
 
     all_y = n_gy * cy
     crow = lax.broadcasted_iota(jnp.int32, (all_y, cz), 0)
@@ -319,23 +340,39 @@
     ratio = left / jnp.maximum(diag_sum, 1.0)
     for i in range(cx):
         whole_corr[i] = e[i] + mask * ratio
-        mine = whole_corr[i, pl.ds(pl.multiple_of(gy * cy, 8), cy), :]
+        corr[1 + i] = whole_corr[i, pl.ds(pl.multiple_of(gy * cy, 8), cy), :]
+    for which, (dx, dy) in enumerate(STEPS):
+        @pl.when(exists(dx, dy))
+        def _():
+            remote_corr(which).start()
+
+    receive(ITERATE)
+    join(ITERATE)
+    for which, (dx, dy) in enumerate(STEPS):
+        @pl.when(exists(-dx, -dy))
+        def _():
+            remote_corr(which).wait_recv()
+
+    for i in range(cx + 2):
+        mine = corr[i]
         spread[i, pl.ds(0, cy, stride=2), :] = mine
         spread[i, pl.ds(1, cy, stride=2), :] = mine
-    for i in range(cx):
-        for r in range(0, ny, 8):
-            tile = spread[i, pl.ds(r, 8), :]
+        for r in range(0, rows, 8):
+            if r < ny:
+                tile = spread[i, pl.ds(r, 8), :]
+            else:
+                tile = jnp.where(
+                    lax.broadcasted_iota(jnp.int32, (8, cz), 0) < HALF,
+                    jnp.broadcast_to(corr_y[0, i, pl.ds(0, 1), :], (8, cz)),
+                    jnp.broadcast_to(corr_y[1, i, pl.ds(7, 1), :], (8, cz)),
+                )
             for part in range(2):
-                wide = jnp.take_along_axis(tile, half_of + 64 * part, axis=1)
-                for j in (first + 2 * i, first + 2 * i + 1):
-                    at = (ITERATE, j, pl.ds(r, 8), pl.ds(128 * part, 128))
-                    ext[at] = ext[at] + wide
-
-    pack(ITERATE)
-    send(ITERATE)
-    receive(ITERATE)
-    join(ITERATE)
-    values = {i: ext[ITERATE, i] for i in range(first - 2, last + 2)}
+                wide[i, pl.ds(r, 8), pl.ds(128 * part, 128)] = jnp.take_along_axis(
+                    tile, half_of + 64 * part, axis=1
+                )
+    values = {
+        i: ext[ITERATE, i] + wide[(i - first + 2) // 2] for i in range(first - 2, last + 2)
+    }
     for sweep in range(POST_SWEEPS):
         reach = POST_SWEEPS - 1 - sweep
         flux = {i: ext[COND, i] * values[i] for i in values}
@@ -351,6 +388,11 @@
 
     for kind in range(3):
         finish(kind)
+    for which, (dx, dy) in enumerate(STEPS):
+        @pl.when(exists(dx, dy))
+        def _():
+            remote_corr(which).wait_send()
+
     for kind in range(2):
         for off in range(1, n_gy):
             gather(kind, off).wait_send()
@@ -386,13 +428,18 @@
             pltpu.VMEM((2, nx // 2, n_gy * ny // 2, nz // 2), f32),
             pltpu.VMEM((nx // 2, ny, nz // 2), f32),
             pltpu.VMEM((nx // 2, n_gy * ny // 2, nz // 2), f32),
-            pltpu.VMEM((nx // 2, ny, nz // 2), f32),
+            pltpu.VMEM((nx // 2 + 2, ny, nz // 2), f32),
+            pltpu.VMEM((nx // 2 + 2, ny // 2, nz // 2), f32),
+            pltpu.VMEM((2, nx // 2 + 2, 8, nz // 2), f32),
+            pltpu.VMEM((nx // 2 + 2, ny + 8, nz), f32),
             pltpu.SemaphoreType.DMA((3, 8)),
             pltpu.SemaphoreType.DMA((3, 8)),
             pltpu.SemaphoreType.DMA((2, n_gy - 1)),
             pltpu.SemaphoreType.DMA((2, n_gy - 1)),
             pltpu.SemaphoreType.DMA((4,)),
             pltpu.SemaphoreType.DMA((nx,)),
+            pltpu.SemaphoreType.DMA((8,)),
+            pltpu.SemaphoreType.DMA((8,)),
         ],
         compiler_params=pltpu.CompilerParams(
             collective_id=0, has_side_effects=True, vmem_limit_bytes=60 * 1024 * 1024

time: 20.4 us -> 20.3 us (level)
  no operation moved by 1% of the time
where the time goes in v4:
time: 20.3 us; the launch traced here: 20.2 us
  Pallas kernels  18.6 us (92%)
  local copies, waits for them, and re-layouts  1.57 us (8%)
    pallas_call x1, Pallas kernels, on_device(): pl.pallas_call(functools.partial(kernel, n_gx, n_gy), out_shape=jax.Shape...  18.6 us
    unnamed x1, local copies, waits for them, and re-layouts  1.57 us

profile of v4, /device:TPU:1, one launch (start us, length us, event | category | flops | bytes accessed | tf_op | source)
XLA Modules:
  0.0 20.2 jit_solution(2661184191357443180)
XLA Ops:
  0.0 18.6 %shard_map.46 = f32[4,32,256]{2,1,0:T(8,128)} custom-call(s32[1,2]{1,0:T(1,128)} %owners_in.1, f32[1,64]{1,0:T(1,128)} %bitcast.1, f32[4,32,256]{2,1,0:T(8,128)} %source_ref.1, s32[4,32,256]{2,1,0:T(8,128)} %region_ref.1), custom_call_target="tpu_custom_call" | custom-call | tf_op jit(solution)/shard_map/pallas_call | solution.py:407
  18.6 1.6 %copy.6 = f32[4,32,256]{2,1,0:T(8,128)} copy(f32[4,32,256]{2,1,0:T(8,128)} %shard_map.46) | data formatting | bytes 262144

commit v5 on v4

--- a/solution.py
+++ b/solution.py
@@ -196,9 +196,10 @@
     z_high = jnp.where(lane == nz - 1, 0.0, 0.5)
     rows = ny + 8
 
-    def blend(a, b, c):
+    def blend(a, b, c, keep=rows):
         u = b + 0.5 * (a + c)
         u = u + 0.5 * (pltpu.roll(u, 1, 0) + pltpu.roll(u, rows - 1, 0))
+        u = u[:keep]
         return u + z_low * pltpu.roll(u, 1, 1) + z_high * pltpu.roll(u, nz - 1, 1)
 
     lane128 = lax.broadcasted_iota(jnp.int32, (8, 128), 1)
@@ -259,9 +260,11 @@
         weight[i] = (in_y * in_x) / (MASS_TERM + 6.0 * cond + mixed)
         diag2[i] = MASS_TERM + 8.0 * cond + mixed
 
-    def defect(kind, i, values, flux):
-        lhs = ext[COND, i] * blend(values[i - 1], values[i], values[i + 1])
-        return ext[SOURCE, i] - diag2[i] * values[i] + lhs + blend(flux[i - 1], flux[i], flux[i + 1])
+    def defect(kind, i, values, flux, keep=rows):
+        at = pl.ds(0, keep)
+        lhs = ext[COND, i, at] * blend(values[i - 1], values[i], values[i + 1], keep)
+        rhs = blend(flux[i - 1], flux[i], flux[i + 1], keep)
+        return ext[SOURCE, i, at] - diag2[i, at] * values[i][:keep] + lhs + rhs
 
     receive(SOURCE)
     join(SOURCE)
@@ -277,7 +280,7 @@
     for i in range(cx):
         j = first + 2 * i
         pairs.append(
-            defect(SOURCE, j, smooth, flux)[:ny] + defect(SOURCE, j + 1, smooth, flux)[:ny]
+            defect(SOURCE, j, smooth, flux, ny) + defect(SOURCE, j + 1, smooth, flux, ny)
         )
     coarsen(pairs, 1)
     for off in range(1, n_gy):
@@ -375,9 +378,10 @@
     }
     for sweep in range(POST_SWEEPS):
         reach = POST_SWEEPS - 1 - sweep
+        keep = rows if reach else ny
         flux = {i: ext[COND, i] * values[i] for i in values}
         values = {
-            i: values[i] + weight[i] * defect(ITERATE, i, values, flux)
+            i: values[i][:keep] + weight[i, pl.ds(0, keep)] * defect(ITERATE, i, values, flux, keep)
             for i in range(first - reach, last + reach)
         }
     stores = []

time: 20.3 us -> 20.4 us (level)
  no operation moved by 1% of the time
where the time goes in v5:
time: 20.4 us; the launch traced here: 20.2 us
  Pallas kernels  18.6 us (91%)
  local copies, waits for them, and re-layouts  1.57 us (8%)
    pallas_call x1, Pallas kernels, on_device(): pl.pallas_call(functools.partial(kernel, n_gx, n_gy), out_shape=jax.Shape...  18.6 us
    unnamed x1, local copies, waits for them, and re-layouts  1.57 us

profile of v5, /device:TPU:1, one launch (start us, length us, event | category | flops | bytes accessed | tf_op | source)
XLA Modules:
  0.0 20.2 jit_solution(10144247485698108715)
XLA Ops:
  0.0 18.6 %shard_map.46 = f32[4,32,256]{2,1,0:T(8,128)} custom-call(s32[1,2]{1,0:T(1,128)} %owners_in.1, f32[1,64]{1,0:T(1,128)} %bitcast.1, f32[4,32,256]{2,1,0:T(8,128)} %source_ref.1, s32[4,32,256]{2,1,0:T(8,128)} %region_ref.1), custom_call_target="tpu_custom_call" | custom-call | tf_op jit(solution)/shard_map/pallas_call | solution.py:411
  18.6 1.6 %copy.6 = f32[4,32,256]{2,1,0:T(8,128)} copy(f32[4,32,256]{2,1,0:T(8,128)} %shard_map.46) | data formatting | bytes 262144

commit v6 on v5

--- a/solution.py
+++ b/solution.py
@@ -23,8 +23,8 @@
 def kernel(
     n_gx, n_gy,
     owners_in, table_in, source_ref, region_ref, out_ref,
-    owners_ref, table_ref, ext, packed, after, before, labels, weight, diag2, result, group, squeezed, whole_corr, spread, corr, corr_y, wide,
-    send_sem, recv_sem, g_send, g_recv, in_sem, out_sem, c_send, c_recv,
+    owners_ref, table_ref, ext, packed, after, before, labels, weight, diag2, group, squeezed, whole_corr, spread, corr, corr_y, wide,
+    send_sem, recv_sem, g_send, g_recv, in_sem, c_send, c_recv,
 ):
     nx, ny, nz = out_ref.shape
     cx, cy, cz = nx // 2, ny // 2, nz // 2
@@ -384,11 +384,8 @@
             i: values[i][:keep] + weight[i, pl.ds(0, keep)] * defect(ITERATE, i, values, flux, keep)
             for i in range(first - reach, last + reach)
         }
-    stores = []
     for i in range(nx):
-        result[i] = values[first + i][:ny]
-        stores.append(pltpu.make_async_copy(result.at[i], out_ref.at[i], out_sem.at[i]))
-        stores[i].start()
+        out_ref[i] = values[first + i][:ny]
 
     for kind in range(3):
         finish(kind)
@@ -400,8 +397,6 @@
     for kind in range(2):
         for off in range(1, n_gy):
             gather(kind, off).wait_send()
-    for store in stores:
-        store.wait()
 
 
 def on_device(source, region, permeability, owners, *, n_gx, n_gy):
@@ -417,7 +412,7 @@
             pl.BlockSpec(memory_space=pltpu.HBM),
             pl.BlockSpec(memory_space=pltpu.HBM),
         ],
-        out_specs=pl.BlockSpec(memory_space=pltpu.HBM),
+        out_specs=pl.BlockSpec(memory_space=pltpu.VMEM),
         scratch_shapes=[
             pltpu.SMEM((1, n_gy), jnp.int32),
             pltpu.VMEM((1, permeability.shape[0]), f32),
@@ -428,7 +423,6 @@
             pltpu.VMEM((nx, ny, nz), jnp.int32),
             pltpu.VMEM((planes, ny + 8, nz), f32),
             pltpu.VMEM((planes, ny + 8, nz), f32),
-            pltpu.VMEM((nx, ny, nz), f32),
             pltpu.VMEM((2, nx // 2, n_gy * ny // 2, nz // 2), f32),
             pltpu.VMEM((nx // 2, ny, nz // 2), f32),
             pltpu.VMEM((nx // 2, n_gy * ny // 2, nz // 2), f32),
@@ -441,12 +435,11 @@
             pltpu.SemaphoreType.DMA((2, n_gy - 1)),
             pltpu.SemaphoreType.DMA((2, n_gy - 1)),
             pltpu.SemaphoreType.DMA((4,)),
-            pltpu.SemaphoreType.DMA((nx,)),
             pltpu.SemaphoreType.DMA((8,)),
             pltpu.SemaphoreType.DMA((8,)),
         ],
         compiler_params=pltpu.CompilerParams(
-            collective_id=0, has_side_effects=True, vmem_limit_bytes=60 * 1024 * 1024
+            collective_id=0, has_side_effects=True, vmem_limit_bytes=56328192
         ),
     )(owners, permeability[None, :], source, region)
 

time: 20.4 us -> 19.5 us (0.956)
  Pallas kernels: 18.6 us -> 18 us
  local copies, waits for them, and re-layouts: 1.57 us -> 1.33 us
    pallas_call x1, Pallas kernels: 18.6 us -> 18 us  [on_device(): pl.pallas_call(functools.partial(kernel, n_gx, n_gy), out_shape=jax.Shape...]
    unnamed x1 -> x5, local copies, waits for them, and re-layouts: 1.57 us -> 1.33 us
where the time goes in v6:
time: 19.5 us; the launch traced here: 19.4 us
  Pallas kernels  18 us (92%)
  local copies, waits for them, and re-layouts  1.33 us (7%)
    pallas_call x1, Pallas kernels, on_device(): pl.pallas_call(functools.partial(kernel, n_gx, n_gy), out_shape=jax.Shape...  18 us
    unnamed x5, local copies, waits for them, and re-layouts  1.33 us

profile of v6, /device:TPU:1, one launch (start us, length us, event | category | flops | bytes accessed | tf_op | source)
XLA Modules:
  0.0 19.4 jit_solution(18432627635847782558)
XLA Ops:
  0.0 0.0 copy-start
  0.0 0.0 copy-start.1
  0.0 0.7 %copy-done = s32[1,2]{1,0:T(1,128)S(1)} copy-done((s32[1,2]{1,0:T(1,128)S(1)}, s32[1,2]{1,0:T(1,128)}, u32[]{:S(2)}) %copy-start) | copy-done | bytes 32
  0.7 0.0 copy-done.1
  0.7 18.0 %shard_map.46 = f32[4,32,256]{2,1,0:T(8,128)S(1)} custom-call(s32[1,2]{1,0:T(1,128)S(1)} %copy-done, f32[1,64]{1,0:T(1,128)S(1)} %bitcast.1, f32[4,32,256]{2,1,0:T(8,128)} %source_ref.1, s32[4,32,256]{2,1,0:T(8,128)} %region_ref.1), custom_call_target="tpu_custom_call" | custom-call | tf_op jit(solution)/shard_map/pallas_call | solution.py:406
  18.7 0.7 %copy.6 = f32[4,32,256]{2,1,0:T(8,128)} copy(f32[4,32,256]{2,1,0:T(8,128)S(1)} %shard_map.46) | data formatting | bytes 262144
Async XLA Ops:
  0.0 0.7 %copy-start = (s32[1,2]{1,0:T(1,128)S(1)}, s32[1,2]{1,0:T(1,128)}, u32[]{:S(2)}) copy-start(s32[1,2]{1,0:T(1,128)} %owners_in.1) | copy-start | bytes 28
  0.0 0.7 %copy-start.1 = (f32[64]{0:T(128)S(1)}, f32[64]{0:T(128)}, u32[]{:S(2)}) copy-start(f32[64]{0:T(128)} %param.6) | copy-start | bytes 772
